TPU v7x, 32 devices: a whole 2x2x4 slice. The times are simulated.
32 devices in a mesh: gx: 2 (over x), gy: 4 (over z), gz: 4 (over y, core).
Axes of the slice: x: 2, y: 2, z: 4, core: 2. Of those that a mesh axis runs over, the one named last changes fastest.
Arguments:
- initial_block: float32 [64, 32, 32, 256], P(None, 'gz', 'gy', 'gx'), may hold values from -6 to 6
- phase_map: int32 [32, 32, 256], P('gz', 'gy', 'gx'), may hold values from 0 to 3
- phase_density: float32 [4], replicated, may hold values from 0.5 to 4
- phase_modulus: float32 [4], replicated, may hold values from 0.5 to 4
- bloch_sign: int32 [32, 256], P('gy', 'gx'), may hold values from -1 to 1, as said below
Outputs:
- ritz_basis: float32 [64, 32, 32, 256], P(None, 'gz', 'gy', 'gx')
- projected: float32 [64, 64], replicated
Inputs may be any that keep to these rules, and one draw needn't show every extreme that they name: `bloch_sign`: each entry is -1 or +1.
All inputs are finite; a program needn't handle non-finite values.
Results may differ from a plain program's by a relative error of at most 0.00011.
Values sent between devices are 32-bit elements; how exact they have to be, the bound alone decides.
A program may use at most 128 MiB of HBM per device.

v0:
```python
import jax
import jax.numpy as jnp
from jax import lax
from jax.sharding import PartitionSpec as P

DEGREE = 6


def extended(block, sides, width):
    for axis, dim in sides:
        count = lax.axis_size(axis)
        forward = [(i, i + 1) for i in range(count - 1)]
        forward.append((count - 1, 0))
        backward = [(target, source) for source, target in forward]
        low = lax.ppermute(
            lax.slice_in_dim(block, block.shape[dim] - width, None, axis=dim), axis, forward
        )
        high = lax.ppermute(lax.slice_in_dim(block, 0, width, axis=dim), axis, backward)
        block = jnp.concatenate([low, block, high], axis=dim)
    return block


def lookup(phase_map, table):
    hits = phase_map[..., None] == jnp.arange(table.shape[0], dtype=jnp.int32)
    return jnp.sum(jnp.where(hits, table, jnp.float32(0.0)), axis=-1)


def gram(left, right):
    rows = left.shape[0]
    return jnp.dot(
        left.reshape(rows, -1), right.reshape(rows, -1).T, precision=lax.Precision.HIGHEST
    )


def stiffness(block, rho_pad, low_factor, high_factor):
    padded = extended(block, (("gx", 3), ("gy", 2), ("gz", 1)), 1)
    padded = padded.at[:, 0, 1:-1, 1:-1].multiply(low_factor[None])
    padded = padded.at[:, -1, 1:-1, 1:-1].multiply(high_factor[None])
    centre = padded[:, 1:-1, 1:-1, 1:-1]
    inv_rho = rho_pad[1:-1, 1:-1, 1:-1]
    w_up = 0.5 * (inv_rho + rho_pad[2:, 1:-1, 1:-1])
    w_down = 0.5 * (inv_rho + rho_pad[:-2, 1:-1, 1:-1])
    total = w_up * (centre - padded[:, 2:, 1:-1, 1:-1]) + w_down * (
        centre - padded[:, :-2, 1:-1, 1:-1]
    )
    w_up = 0.5 * (inv_rho + rho_pad[1:-1, 2:, 1:-1])
    w_down = 0.5 * (inv_rho + rho_pad[1:-1, :-2, 1:-1])
    total = total + (
        w_up * (centre - padded[:, 1:-1, 2:, 1:-1]) + w_down * (centre - padded[:, 1:-1, :-2, 1:-1])
    )
    w_up = 0.5 * (inv_rho + rho_pad[1:-1, 1:-1, 2:])
    w_down = 0.5 * (inv_rho + rho_pad[1:-1, 1:-1, :-2])
    total = total + (
        w_up * (centre - padded[:, 1:-1, 1:-1, 2:]) + w_down * (centre - padded[:, 1:-1, 1:-1, :-2])
    )
    return total


def body(initial_block, phase_map, phase_density, phase_modulus, bloch_sign):
    inv_rho = lookup(phase_map, 1.0 / phase_density)
    kappa = lookup(phase_map, phase_modulus)
    sign = bloch_sign.astype(jnp.float32)
    z_index = lax.axis_index("gz")
    z_count = lax.axis_size("gz")
    low_factor = jnp.where(z_index == 0, sign, jnp.float32(1.0))
    high_factor = jnp.where(z_index == z_count - 1, sign, jnp.float32(1.0))
    rho_pad = extended(inv_rho, (("gx", 2), ("gy", 1), ("gz", 0)), 1)
    top = 12.0 * jnp.max(phase_modulus) * jnp.max(1.0 / phase_density)
    low = 0.03 * top
    centre = (top + low) / 2.0
    half = (top - low) / 2.0
    cells = (
        initial_block.shape[1]
        * initial_block.shape[2]
        * initial_block.shape[3]
        * lax.axis_size("gx")
        * lax.axis_size("gy")
        * z_count
    )
    current = initial_block
    lap = kappa * stiffness(current, rho_pad, low_factor, high_factor)
    following = (lap - centre * current) / half
    previous, current = (current, following)
    for step in range(DEGREE - 1):
        lap = kappa * stiffness(current, rho_pad, low_factor, high_factor)
        following = 2.0 * (lap - centre * current) / half - previous
        previous, current = (current, following)
    correlation_local = gram(current / kappa[None], current)
    applied = stiffness(current, rho_pad, low_factor, high_factor)
    energy_local = gram(current, applied)
    correlation_total, energy_total = lax.psum(
        (correlation_local, energy_local), ("gx", "gy", "gz")
    )
    correlation = correlation_total / cells
    energy = energy_total / cells
    rows = current.shape[0]
    factor = jnp.linalg.cholesky(correlation)
    inverse = jax.scipy.linalg.solve_triangular(
        factor, jnp.eye(rows, dtype=jnp.float32), lower=True
    )
    basis = jnp.dot(inverse, current.reshape(rows, -1), precision=lax.Precision.HIGHEST).reshape(
        current.shape
    )
    projected = jnp.dot(
        jnp.dot(inverse, energy, precision=lax.Precision.HIGHEST),
        inverse.T,
        precision=lax.Precision.HIGHEST,
    )
    return (basis, projected)


def solution(mesh):
    in_specs = (P(None, "gz", "gy", "gx"), P("gz", "gy", "gx"), P(), P(), P("gy", "gx"))
    out_specs = (P(None, "gz", "gy", "gx"), P())
    return jax.shard_map(body, mesh=mesh, in_specs=in_specs, out_specs=out_specs, check_vma=False)
```

profile of v0, /device:TPU:0, one launch (start us, length us, event | category | flops | bytes accessed | tf_op | source)
XLA Modules:
  0.0 1980.2 jit_solution(10078879603563903501)
XLA Ops:
  88.8 86.9 %scatter-mul.46 = f32[64,10,10,130]{3,1,2,0:T(8,128)} dynamic-update-slice(f32[64,10,10,130]{3,1,2,0:T(8,128)} %pad_maximum_fusion, f32[64,1,8,128]{3,1,2,0:T(1,128)} %copy.195, s32[]{:T(128)} %constant.380.clone.1, s32[]{:T(128)} %constant.380.clone.1, s32[]{:T(128)} %constant.381.clone.1, s32[]{:T(128)} %constant.381.clone.1) | dynamic-update-slice | bytes 524292 | tf_op jit(solution)/shard_map/scatter-mul | solution.py:37
  178.5 87.5 %scatter-mul.49 = f32[64,10,10,130]{3,1,2,0:T(8,128)} dynamic-update-slice(f32[64,10,10,130]{3,1,2,0:T(8,128)} %scatter-mul.46, f32[64,1,8,128]{3,1,2,0:T(1,128)S(1)} %slice_multiply_fusion.12, s32[]{:T(128)} %constant.380.clone.1, s32[]{:T(128)} %constant.383.clone.1, s32[]{:T(128)} %constant.381.clone.1, s32[]{:T(128)} %constant.381.clone.1) | dynamic-update-slice | bytes 524292 | tf_op jit(solution)/shard_map/scatter-mul | solution.py:38
  266.0 19.6 fusion.96
  357.8 87.4 %scatter-mul.50 = f32[64,10,10,130]{3,1,2,0:T(8,128)} dynamic-update-slice(f32[64,10,10,130]{3,1,2,0:T(8,128)} %pad_maximum_fusion.1, f32[64,1,8,128]{3,1,2,0:T(1,128)S(1)} %copy.211, s32[]{:T(128)} %constant.380.clone.1, s32[]{:T(128)} %constant.380.clone.1, s32[]{:T(128)} %constant.381.clone.1, s32[]{:T(128)} %constant.381.clone.1) | dynamic-update-slice | bytes 524292 | tf_op jit(solution)/shard_map/scatter-mul | solution.py:37
  448.1 87.5 %scatter-mul.51 = f32[64,10,10,130]{3,1,2,0:T(8,128)} dynamic-update-slice(f32[64,10,10,130]{3,1,2,0:T(8,128)} %scatter-mul.50, f32[64,1,8,128]{3,1,2,0:T(1,128)S(1)} %slice_multiply_fusion.10, s32[]{:T(128)} %constant.380.clone.1, s32[]{:T(128)} %constant.383.clone.1, s32[]{:T(128)} %constant.381.clone.1, s32[]{:T(128)} %constant.381.clone.1) | dynamic-update-slice | bytes 524292 | tf_op jit(solution)/shard_map/scatter-mul | solution.py:38
  535.6 20.8 %fusion.82 = f32[64,8,8,128]{3,1,2,0:T(8,128)} fusion(f32[64,10,10,130]{3,1,2,0:T(8,128)} %scatter-mul.51, f32[64,8,8,128]{3,1,2,0:T(8,128)S(1)} %fusion.96, f32[]{:T(128)S(6)} %div.58, f32[]{:T(128)S(6)} %div.57, f32[8,8,128]{2,0,1:T(8,128)S(1)} %copy.200, f32[8,8,128]{2,0,1:T(8,128)S(1)} %copy.199, f32[8,8,128]{2,0,1:T(8,128)S(1)} %copy.198, ...), kind=kLoop, calls=%fused_computation.121 | loop fusion | flops 12058624 | bytes 21200904 | tf_op jit(solution)/shard_map/sub | solution.py:86
  630.2 87.4 %scatter-mul.54 = f32[64,10,10,130]{3,1,2,0:T(8,128)} dynamic-update-slice(f32[64,10,10,130]{3,1,2,0:T(8,128)} %pad_maximum_fusion.2, f32[64,1,8,128]{3,1,2,0:T(1,128)S(1)} %copy.222, s32[]{:T(128)} %constant.380.clone.1, s32[]{:T(128)} %constant.380.clone.1, s32[]{:T(128)} %constant.381.clone.1, s32[]{:T(128)} %constant.381.clone.1) | dynamic-update-slice | bytes 524292 | tf_op jit(solution)/shard_map/scatter-mul | solution.py:37
  720.4 87.5 %scatter-mul.55 = f32[64,10,10,130]{3,1,2,0:T(8,128)} dynamic-update-slice(f32[64,10,10,130]{3,1,2,0:T(8,128)} %scatter-mul.54, f32[64,1,8,128]{3,1,2,0:T(1,128)S(1)} %slice_multiply_fusion.8, s32[]{:T(128)} %constant.380.clone.1, s32[]{:T(128)} %constant.383.clone.1, s32[]{:T(128)} %constant.381.clone.1, s32[]{:T(128)} %constant.381.clone.1) | dynamic-update-slice | bytes 524292 | tf_op jit(solution)/shard_map/scatter-mul | solution.py:38
  807.9 21.0 %fusion.66 = f32[64,8,8,128]{3,1,2,0:T(8,128)} fusion(f32[64,8,8,128]{3,1,2,0:T(8,128)S(1)} %fusion.96, f32[64,10,10,130]{3,1,2,0:T(8,128)} %scatter-mul.55, f32[64,8,8,128]{3,1,2,0:T(8,128)} %fusion.82, f32[]{:T(128)S(6)} %div.58, f32[]{:T(128)S(6)} %div.57, f32[8,8,128]{2,0,1:T(8,128)S(1)} %copy.200, f32[8,8,128]{2,0,1:T(8,128)S(1)} %copy.199, ...), kind=kLoop, calls=%fused_computation.99 | loop fusion | flops 12058624 | bytes 21200904 | tf_op jit(solution)/shard_map/sub | solution.py:86
  902.1 87.4 %scatter-mul.56 = f32[64,10,10,130]{3,1,2,0:T(8,128)} dynamic-update-slice(f32[64,10,10,130]{3,1,2,0:T(8,128)} %pad_maximum_fusion.3, f32[64,1,8,128]{3,1,2,0:T(1,128)S(1)} %copy.232, s32[]{:T(128)} %constant.380.clone.1, s32[]{:T(128)} %constant.380.clone.1, s32[]{:T(128)} %constant.381.clone.1, s32[]{:T(128)} %constant.381.clone.1) | dynamic-update-slice | bytes 524292 | tf_op jit(solution)/shard_map/scatter-mul | solution.py:37
  992.4 87.5 %scatter-mul.59 = f32[64,10,10,130]{3,1,2,0:T(8,128)} dynamic-update-slice(f32[64,10,10,130]{3,1,2,0:T(8,128)} %scatter-mul.56, f32[64,1,8,128]{3,1,2,0:T(1,128)S(1)} %slice_multiply_fusion.6, s32[]{:T(128)} %constant.380.clone.1, s32[]{:T(128)} %constant.383.clone.1, s32[]{:T(128)} %constant.381.clone.1, s32[]{:T(128)} %constant.381.clone.1) | dynamic-update-slice | bytes 524292 | tf_op jit(solution)/shard_map/scatter-mul | solution.py:38
  1079.9 20.8 %fusion.50 = f32[64,8,8,128]{3,1,2,0:T(8,128)S(1)} fusion(f32[64,8,8,128]{3,1,2,0:T(8,128)} %fusion.82, f32[64,10,10,130]{3,1,2,0:T(8,128)} %scatter-mul.59, f32[64,8,8,128]{3,1,2,0:T(8,128)} %fusion.66, f32[]{:T(128)S(6)} %div.58, f32[]{:T(128)S(6)} %div.57, f32[8,8,128]{2,0,1:T(8,128)S(1)} %copy.200, f32[8,8,128]{2,0,1:T(8,128)S(1)} %copy.199, ...), kind=kLoop, calls=%fused_computation.77 | loop fusion | flops 12058624 | bytes 21200904 | tf_op jit(solution)/shard_map/sub | solution.py:86
  1150.7 13.5 collective-permute-done.34
  1173.0 87.4 %scatter-mul.60 = f32[64,10,10,130]{3,1,2,0:T(8,128)} dynamic-update-slice(f32[64,10,10,130]{3,1,2,0:T(8,128)} %pad_maximum_fusion.4, f32[64,1,8,128]{3,1,2,0:T(1,128)S(1)} %copy.242, s32[]{:T(128)} %constant.380.clone.1, s32[]{:T(128)} %constant.380.clone.1, s32[]{:T(128)} %constant.381.clone.1, s32[]{:T(128)} %constant.381.clone.1) | dynamic-update-slice | bytes 524292 | tf_op jit(solution)/shard_map/scatter-mul | solution.py:37
  1263.3 87.5 %scatter-mul.61 = f32[64,10,10,130]{3,1,2,0:T(8,128)} dynamic-update-slice(f32[64,10,10,130]{3,1,2,0:T(8,128)} %scatter-mul.60, f32[64,1,8,128]{3,1,2,0:T(1,128)S(1)} %slice_multiply_fusion.4, s32[]{:T(128)} %constant.380.clone.1, s32[]{:T(128)} %constant.383.clone.1, s32[]{:T(128)} %constant.381.clone.1, s32[]{:T(128)} %constant.381.clone.1) | dynamic-update-slice | bytes 524292 | tf_op jit(solution)/shard_map/scatter-mul | solution.py:38
  1350.8 20.6 %fusion.34 = f32[64,8,8,128]{3,1,2,0:T(8,128)} fusion(f32[64,8,8,128]{3,1,2,0:T(8,128)} %fusion.66, f32[64,10,10,130]{3,1,2,0:T(8,128)} %scatter-mul.61, f32[64,8,8,128]{3,1,2,0:T(8,128)S(1)} %fusion.50, f32[]{:T(128)S(6)} %div.58, f32[]{:T(128)S(6)} %div.57, f32[8,8,128]{2,0,1:T(8,128)S(1)} %copy.200, f32[8,8,128]{2,0,1:T(8,128)S(1)} %copy.199, ...), kind=kLoop, calls=%fused_computation.55 | loop fusion | flops 12058624 | bytes 21200904 | tf_op jit(solution)/shard_map/sub | solution.py:86
  1420.9 13.5 collective-permute-done.40
  1443.5 87.4 %scatter-mul.64 = f32[64,10,10,130]{3,1,2,0:T(8,128)} dynamic-update-slice(f32[64,10,10,130]{3,1,2,0:T(8,128)} %pad_maximum_fusion.5, f32[64,1,8,128]{3,1,2,0:T(1,128)S(1)} %copy.252, s32[]{:T(128)} %constant.380.clone.1, s32[]{:T(128)} %constant.380.clone.1, s32[]{:T(128)} %constant.381.clone.1, s32[]{:T(128)} %constant.381.clone.1) | dynamic-update-slice | bytes 524292 | tf_op jit(solution)/shard_map/scatter-mul | solution.py:37
  1533.7 87.5 %scatter-mul.65 = f32[64,10,10,130]{3,1,2,0:T(8,128)} dynamic-update-slice(f32[64,10,10,130]{3,1,2,0:T(8,128)} %scatter-mul.64, f32[64,1,8,128]{3,1,2,0:T(1,128)S(1)} %slice_multiply_fusion.2, s32[]{:T(128)} %constant.380.clone.1, s32[]{:T(128)} %constant.383.clone.1, s32[]{:T(128)} %constant.381.clone.1, s32[]{:T(128)} %constant.381.clone.1) | dynamic-update-slice | bytes 524292 | tf_op jit(solution)/shard_map/scatter-mul | solution.py:38
  1621.2 21.8 %broadcast_divide_fusion = (f32[64,8,8,128]{3,1,2,0:T(8,128)}, f32[64,8,8,128]{3,1,2,0:T(8,128)S(1)}) fusion(f32[8,8,128]{2,0,1:T(8,128)S(1)} %copy.183, f32[64,8,8,128]{3,1,2,0:T(8,128)} %copy-done, f32[]{:T(128)S(6)} %div.58, f32[64,8,8,128]{3,1,2,0:T(8,128)} %fusion.34, f32[]{:T(128)S(6)} %div.57, f32[64,10,10,130]{3,1,2,0:T(8,128)} %scatter-mul.65, ...), kind=kLoop, calls=%fused_computation.165 | loop fusion | flops 12582912 | bytes 23298056 | tf_op jit(solution)/shard_map/div | solution.py:88
  1714.9 87.4 %scatter-mul.66 = f32[64,10,10,130]{3,1,2,0:T(8,128)} dynamic-update-slice(f32[64,10,10,130]{3,1,2,0:T(8,128)} %pad_maximum_fusion.6, f32[64,1,8,128]{3,1,2,0:T(1,128)S(1)} %copy.268, s32[]{:T(128)} %constant.380.clone.1, s32[]{:T(128)} %constant.380.clone.1, s32[]{:T(128)} %constant.381.clone.1, s32[]{:T(128)} %constant.381.clone.1) | dynamic-update-slice | bytes 524292 | tf_op jit(solution)/shard_map/scatter-mul | solution.py:37
  1805.2 87.5 %scatter-mul.69 = f32[64,10,10,130]{3,1,2,0:T(8,128)} dynamic-update-slice(f32[64,10,10,130]{3,1,2,0:T(8,128)} %scatter-mul.66, f32[64,1,8,128]{3,1,2,0:T(1,128)S(1)} %slice_multiply_fusion, s32[]{:T(128)} %constant.380.clone.1, s32[]{:T(128)} %constant.383.clone.1, s32[]{:T(128)} %constant.381.clone.1, s32[]{:T(128)} %constant.381.clone.1) | dynamic-update-slice | bytes 524292 | tf_op jit(solution)/shard_map/scatter-mul | solution.py:38
  1892.6 19.9 %fusion.2 = f32[64,8,8,128]{3,1,2,0:T(8,128)} fusion(f32[64,10,10,130]{3,1,2,0:T(8,128)} %scatter-mul.69, f32[8,8,128]{2,0,1:T(8,128)S(1)} %copy.200, f32[8,8,128]{2,0,1:T(8,128)S(1)} %copy.199, f32[8,8,128]{2,0,1:T(8,128)S(1)} %copy.198, f32[8,8,128]{2,0,1:T(8,128)S(1)} %copy.197, f32[8,8,128]{2,0,1:T(8,128)S(1)} %copy.196, f32[8,8,128]{2,0,1:T(8,128)S(1)} %copy.184), kind=kLoop, calls=%fused_computation.11 | loop fusion | flops 8912896 | bytes 16973824 | tf_op jit(solution)/shard_map/add | solution.py:53
  1918.2 41.0 %all-reduce = (f32[64,64]{0,1:T(8,128)S(1)}, f32[64,64]{0,1:T(8,128)S(1)}) all-reduce(f32[64,64]{0,1:T(8,128)S(1)} %fusion.113, f32[64,64]{0,1:T(8,128)S(1)} %fusion.118), channel_id=1, replica_groups=mesh['gx'=2,'gy'=4,'gz'=4] {'gx','gy','gz'}, use_global_device_ids=true, to_apply=%region_4.5 | all-reduce | flops 8192 | bytes 65536 | tf_op jit(solution)/shard_map/psum | solution.py:91
  (280 shorter events, 540.5 us)
Async XLA Ops:
  2.8 17.3 collective-permute-start.1
  20.3 18.4 collective-permute-start.3
  32.9 16.9 collective-permute-start.7
  32.9 23.7 %collective-permute-start.8 = (f32[64,8,1,130]{3,1,2,0:T(8,128)}, f32[64,8,1,130]{3,1,2,0:T(8,128)S(1)}, u32[]{:S(2)}, u32[]{:S(2)}) collective-permute-start(f32[64,8,1,130]{3,1,2,0:T(8,128)} %get-tuple-element.215), channel_id=1, source_target_pairs={{4,0},{8,4},{12,8},{0,12},{5,1},{9,5},{13,9},{1,13},{6,2},{10,6},{... | collective-permute-start | bytes 798728 | tf_op jit(solution)/shard_map/ppermute | solution.py:18
  38.8 27.7 %collective-permute-start.4 = (f32[1,10,130]{2,1,0:T(8,128)S(1)}, f32[1,10,130]{2,1,0:T(8,128)S(1)}, u32[]{:S(2)}, u32[]{:S(2)}) collective-permute-start(f32[1,10,130]{2,1,0:T(8,128)S(1)} %get-tuple-element.232), channel_id=1, source_target_pairs={{1,0},{2,1},{3,2},{0,3},{5,4},{6,5},{7,6},{4,7},{9,8},{10,9},{11,1... | collective-permute-start | bytes 15608 | tf_op jit(solution)/shard_map/ppermute | solution.py:18
  38.8 27.7 %collective-permute-start.11 = (f32[1,10,130]{2,1,0:T(8,128)S(1)}, f32[1,10,130]{2,1,0:T(8,128)S(1)}, u32[]{:S(2)}, u32[]{:S(2)}) collective-permute-start(f32[1,10,130]{2,1,0:T(8,128)S(1)} %get-tuple-element.233), channel_id=1, source_target_pairs={{0,1},{1,2},{2,3},{3,0},{4,5},{5,6},{6,7},{7,4},{8,9},{9,10},{10,1... | collective-permute-start | bytes 15608 | tf_op jit(solution)/shard_map/ppermute | solution.py:15
  64.7 16.4 collective-permute-start.10
  303.7 16.8 collective-permute-start.14
  306.1 23.7 %collective-permute-start.15 = (f32[64,8,1,130]{3,1,2,0:T(8,128)S(1)}, f32[64,8,1,130]{3,1,2,0:T(8,128)S(1)}, u32[]{:S(2)}, u32[]{:S(2)}) collective-permute-start(f32[64,8,1,130]{3,1,2,0:T(8,128)S(1)} %get-tuple-element.213), channel_id=1, source_target_pairs={{4,0},{8,4},{12,8},{0,12},{5,1},{9,5},{13,9},{1,13},{6,2},{10,6},{... | collective-permute-start | bytes 798728 | tf_op jit(solution)/shard_map/ppermute | solution.py:18
  334.2 16.1 collective-permute-start.17
  576.9 16.7 collective-permute-start.20
  577.5 24.4 %collective-permute-start.21 = (f32[64,8,1,130]{3,1,2,0:T(8,128)S(1)}, f32[64,8,1,130]{3,1,2,0:T(8,128)S(1)}, u32[]{:S(2)}, u32[]{:S(2)}) collective-permute-start(f32[64,8,1,130]{3,1,2,0:T(8,128)S(1)} %get-tuple-element.211), channel_id=1, source_target_pairs={{4,0},{8,4},{12,8},{0,12},{5,1},{9,5},{13,9},{1,13},{6,2},{10,6},{... | collective-permute-start | bytes 798728 | tf_op jit(solution)/shard_map/ppermute | solution.py:18
  847.5 16.7 collective-permute-start.26
  848.8 24.6 %collective-permute-start.27 = (f32[64,8,1,130]{3,1,2,0:T(8,128)S(1)}, f32[64,8,1,130]{3,1,2,0:T(8,128)S(1)}, u32[]{:S(2)}, u32[]{:S(2)}) collective-permute-start(f32[64,8,1,130]{3,1,2,0:T(8,128)S(1)} %get-tuple-element.209), channel_id=1, source_target_pairs={{4,0},{8,4},{12,8},{0,12},{5,1},{9,5},{13,9},{1,13},{6,2},{10,6},{... | collective-permute-start | bytes 798728 | tf_op jit(solution)/shard_map/ppermute | solution.py:18
  877.8 16.4 collective-permute-start.29
  1118.9 16.7 collective-permute-start.32
  1120.4 24.1 %collective-permute-start.33 = (f32[64,8,1,130]{3,1,2,0:T(8,128)S(1)}, f32[64,8,1,130]{3,1,2,0:T(8,128)S(1)}, u32[]{:S(2)}, u32[]{:S(2)}) collective-permute-start(f32[64,8,1,130]{3,1,2,0:T(8,128)S(1)} %get-tuple-element.207), channel_id=1, source_target_pairs={{4,0},{8,4},{12,8},{0,12},{5,1},{9,5},{13,9},{1,13},{6,2},{10,6},{... | collective-permute-start | bytes 798728 | tf_op jit(solution)/shard_map/ppermute | solution.py:18
  1148.9 16.4 collective-permute-start.35
  1390.0 16.7 collective-permute-start.38
  1390.7 24.0 %collective-permute-start.39 = (f32[64,8,1,130]{3,1,2,0:T(8,128)S(1)}, f32[64,8,1,130]{3,1,2,0:T(8,128)S(1)}, u32[]{:S(2)}, u32[]{:S(2)}) collective-permute-start(f32[64,8,1,130]{3,1,2,0:T(8,128)S(1)} %get-tuple-element.205), channel_id=1, source_target_pairs={{4,0},{8,4},{12,8},{0,12},{5,1},{9,5},{13,9},{1,13},{6,2},{10,6},{... | collective-permute-start | bytes 798728 | tf_op jit(solution)/shard_map/ppermute | solution.py:18
  1419.1 16.4 collective-permute-start.41
  1661.2 16.7 collective-permute-start.44
  1662.4 24.1 %collective-permute-start.45 = (f32[64,8,1,130]{3,1,2,0:T(8,128)S(1)}, f32[64,8,1,130]{3,1,2,0:T(8,128)S(1)}, u32[]{:S(2)}, u32[]{:S(2)}) collective-permute-start(f32[64,8,1,130]{3,1,2,0:T(8,128)S(1)} %get-tuple-element.203), channel_id=1, source_target_pairs={{4,0},{8,4},{12,8},{0,12},{5,1},{9,5},{13,9},{1,13},{6,2},{10,6},{... | collective-permute-start | bytes 798728 | tf_op jit(solution)/shard_map/ppermute | solution.py:18
  1690.9 16.2 collective-permute-start.47
  (47 other events, 903.4 us)
where the time goes:
time: 1990 us; the launch traced here: 1980 us
  local copies, waits for them, and re-layouts  1350 us (68%)
  other arithmetic  277 us (14%)
  waiting for transfers between devices  234 us (12%)
  starting transfers between devices  62.9 us (3%)
  blocking collectives  41 us (2%)
    another operation x7, local copies, waits for them, and re-layouts, stiffness(): padded = padded.at[:, -1, 1:-1, 1:-1].multiply(high_factor[None])  612 us
    another operation x7, local copies, waits for them, and re-layouts, stiffness(): padded = padded.at[:, 0, 1:-1, 1:-1].multiply(low_factor[None])  612 us
    ppermute x24, waiting for transfers between devices, extended(): lax.ppermute(lax.slice_in_dim(block, block.shape[dim] - width, None, axis...  173 us
    sub x4, other arithmetic, body(): following = 2.0 * (lap - centre * current) / half - previous  83.2 us
    ppermute x24, waiting for transfers between devices, extended(): lax.ppermute(lax.slice_in_dim(block, 0, width, axis=dim), axis, backward)  61 us
    concatenate x8, other arithmetic, extended(): block = jnp.concatenate([low, block, high], axis=dim)  49.4 us
    slice x14, other arithmetic, extended(): lax.slice_in_dim(block, block.shape[dim] - width, None, axis=dim)  46.8 us
    ppermute x24, starting transfers between devices, extended(): lax.ppermute(lax.slice_in_dim(block, 0, width, axis=dim), axis, backward)  45 us
  transfers between devices with their start and end apart: 48, of which 27 were waited for; matrix products, arithmetic and copies ran while one was open for 4% of the time, Pallas kernels for 0%

commit v1 on v0

--- a/solution.py
+++ b/solution.py
@@ -88,8 +88,8 @@
     correlation_local = gram(current / kappa[None], current)
     applied = stiffness(current, rho_pad, low_factor, high_factor)
     energy_local = gram(current, applied)
-    correlation_total, energy_total = lax.psum(
-        (correlation_local, energy_local), ("gx", "gy", "gz")
+    correlation_total, energy_total = jax.lax.psum(
+        jax.lax.psum((correlation_local, energy_local), ("gy", "gz")), "gx"
     )
     correlation = correlation_total / cells
     energy = energy_total / cells

time: 1990 us -> 2010 us (1.010)
  blocking collectives: 41 us -> 69.6 us
    psum x1 -> x2, blocking collectives: 41 us -> 69.6 us  [the longest x1 60.5 us: body(): jax.lax.psum((correlation_local, energy_local), ('gy', 'gz'))]
where the time goes in v1:
time: 2010 us; the launch traced here: 2000 us
  local copies, waits for them, and re-layouts  1350 us (67%)
  other arithmetic  272 us (14%)
  waiting for transfers between devices  234 us (12%)
  blocking collectives  69.6 us (3%)
  starting transfers between devices  62.9 us (3%)
    another operation x7, local copies, waits for them, and re-layouts, stiffness(): padded = padded.at[:, -1, 1:-1, 1:-1].multiply(high_factor[None])  612 us
    another operation x7, local copies, waits for them, and re-layouts, stiffness(): padded = padded.at[:, 0, 1:-1, 1:-1].multiply(low_factor[None])  612 us
    ppermute x24, waiting for transfers between devices, extended(): lax.ppermute(lax.slice_in_dim(block, block.shape[dim] - width, None, axis...  173 us
    sub x4, other arithmetic, body(): following = 2.0 * (lap - centre * current) / half - previous  80.8 us
    ppermute x24, waiting for transfers between devices, extended(): lax.ppermute(lax.slice_in_dim(block, 0, width, axis=dim), axis, backward)  61 us
    psum x1, blocking collectives, body(): jax.lax.psum((correlation_local, energy_local), ('gy', 'gz'))  60.5 us
    concatenate x8, other arithmetic, extended(): block = jnp.concatenate([low, block, high], axis=dim)  49.3 us
    slice x14, other arithmetic, extended(): lax.slice_in_dim(block, block.shape[dim] - width, None, axis=dim)  46.7 us
  transfers between devices with their start and end apart: 48, of which 27 were waited for; matrix products, arithmetic and copies ran while one was open for 4% of the time, Pallas kernels for 0%

profile of v1, /device:TPU:0, one launch (start us, length us, event | category | flops | bytes accessed | tf_op | source)
XLA Modules:
  0.0 2004.5 jit_solution(6943103890492906240)
XLA Ops:
  88.7 86.9 %scatter-mul.46 = f32[64,10,10,130]{3,1,2,0:T(8,128)} dynamic-update-slice(f32[64,10,10,130]{3,1,2,0:T(8,128)} %pad_maximum_fusion, f32[64,1,8,128]{3,1,2,0:T(1,128)} %copy.195, s32[]{:T(128)} %constant.380.clone.1, s32[]{:T(128)} %constant.380.clone.1, s32[]{:T(128)} %constant.381.clone.1, s32[]{:T(128)} %constant.381.clone.1) | dynamic-update-slice | bytes 524292 | tf_op jit(solution)/shard_map/scatter-mul | solution.py:37
  178.5 87.5 %scatter-mul.49 = f32[64,10,10,130]{3,1,2,0:T(8,128)} dynamic-update-slice(f32[64,10,10,130]{3,1,2,0:T(8,128)} %scatter-mul.46, f32[64,1,8,128]{3,1,2,0:T(1,128)S(1)} %slice_multiply_fusion.12, s32[]{:T(128)} %constant.380.clone.1, s32[]{:T(128)} %constant.383.clone.1, s32[]{:T(128)} %constant.381.clone.1, s32[]{:T(128)} %constant.381.clone.1) | dynamic-update-slice | bytes 524292 | tf_op jit(solution)/shard_map/scatter-mul | solution.py:38
  266.0 19.0 fusion.96
  357.2 87.4 %scatter-mul.50 = f32[64,10,10,130]{3,1,2,0:T(8,128)} dynamic-update-slice(f32[64,10,10,130]{3,1,2,0:T(8,128)} %pad_maximum_fusion.1, f32[64,1,8,128]{3,1,2,0:T(1,128)S(1)} %copy.211, s32[]{:T(128)} %constant.380.clone.1, s32[]{:T(128)} %constant.380.clone.1, s32[]{:T(128)} %constant.381.clone.1, s32[]{:T(128)} %constant.381.clone.1) | dynamic-update-slice | bytes 524292 | tf_op jit(solution)/shard_map/scatter-mul | solution.py:37
  447.5 87.5 %scatter-mul.51 = f32[64,10,10,130]{3,1,2,0:T(8,128)} dynamic-update-slice(f32[64,10,10,130]{3,1,2,0:T(8,128)} %scatter-mul.50, f32[64,1,8,128]{3,1,2,0:T(1,128)S(1)} %slice_multiply_fusion.10, s32[]{:T(128)} %constant.380.clone.1, s32[]{:T(128)} %constant.383.clone.1, s32[]{:T(128)} %constant.381.clone.1, s32[]{:T(128)} %constant.381.clone.1) | dynamic-update-slice | bytes 524292 | tf_op jit(solution)/shard_map/scatter-mul | solution.py:38
  534.9 20.2 %fusion.82 = f32[64,8,8,128]{3,1,2,0:T(8,128)} fusion(f32[64,10,10,130]{3,1,2,0:T(8,128)} %scatter-mul.51, f32[64,8,8,128]{3,1,2,0:T(8,128)S(1)} %fusion.96, f32[]{:T(128)S(6)} %div.58, f32[]{:T(128)S(6)} %div.57, f32[8,8,128]{2,0,1:T(8,128)S(1)} %copy.200, f32[8,8,128]{2,0,1:T(8,128)S(1)} %copy.199, f32[8,8,128]{2,0,1:T(8,128)S(1)} %copy.198, ...), kind=kLoop, calls=%fused_computation.121 | loop fusion | flops 12058624 | bytes 21200904 | tf_op jit(solution)/shard_map/sub | solution.py:86
  629.0 87.4 %scatter-mul.54 = f32[64,10,10,130]{3,1,2,0:T(8,128)} dynamic-update-slice(f32[64,10,10,130]{3,1,2,0:T(8,128)} %pad_maximum_fusion.2, f32[64,1,8,128]{3,1,2,0:T(1,128)S(1)} %copy.222, s32[]{:T(128)} %constant.380.clone.1, s32[]{:T(128)} %constant.380.clone.1, s32[]{:T(128)} %constant.381.clone.1, s32[]{:T(128)} %constant.381.clone.1) | dynamic-update-slice | bytes 524292 | tf_op jit(solution)/shard_map/scatter-mul | solution.py:37
  719.3 87.5 %scatter-mul.55 = f32[64,10,10,130]{3,1,2,0:T(8,128)} dynamic-update-slice(f32[64,10,10,130]{3,1,2,0:T(8,128)} %scatter-mul.54, f32[64,1,8,128]{3,1,2,0:T(1,128)S(1)} %slice_multiply_fusion.8, s32[]{:T(128)} %constant.380.clone.1, s32[]{:T(128)} %constant.383.clone.1, s32[]{:T(128)} %constant.381.clone.1, s32[]{:T(128)} %constant.381.clone.1) | dynamic-update-slice | bytes 524292 | tf_op jit(solution)/shard_map/scatter-mul | solution.py:38
  806.8 20.3 %fusion.66 = f32[64,8,8,128]{3,1,2,0:T(8,128)} fusion(f32[64,8,8,128]{3,1,2,0:T(8,128)S(1)} %fusion.96, f32[64,10,10,130]{3,1,2,0:T(8,128)} %scatter-mul.55, f32[64,8,8,128]{3,1,2,0:T(8,128)} %fusion.82, f32[]{:T(128)S(6)} %div.58, f32[]{:T(128)S(6)} %div.57, f32[8,8,128]{2,0,1:T(8,128)S(1)} %copy.200, f32[8,8,128]{2,0,1:T(8,128)S(1)} %copy.199, ...), kind=kLoop, calls=%fused_computation.99 | loop fusion | flops 12058624 | bytes 21200904 | tf_op jit(solution)/shard_map/sub | solution.py:86
  877.8 13.5 collective-permute-done.28
  900.3 87.4 %scatter-mul.56 = f32[64,10,10,130]{3,1,2,0:T(8,128)} dynamic-update-slice(f32[64,10,10,130]{3,1,2,0:T(8,128)} %pad_maximum_fusion.3, f32[64,1,8,128]{3,1,2,0:T(1,128)S(1)} %copy.232, s32[]{:T(128)} %constant.380.clone.1, s32[]{:T(128)} %constant.380.clone.1, s32[]{:T(128)} %constant.381.clone.1, s32[]{:T(128)} %constant.381.clone.1) | dynamic-update-slice | bytes 524292 | tf_op jit(solution)/shard_map/scatter-mul | solution.py:37
  990.6 87.5 %scatter-mul.59 = f32[64,10,10,130]{3,1,2,0:T(8,128)} dynamic-update-slice(f32[64,10,10,130]{3,1,2,0:T(8,128)} %scatter-mul.56, f32[64,1,8,128]{3,1,2,0:T(1,128)S(1)} %slice_multiply_fusion.6, s32[]{:T(128)} %constant.380.clone.1, s32[]{:T(128)} %constant.383.clone.1, s32[]{:T(128)} %constant.381.clone.1, s32[]{:T(128)} %constant.381.clone.1) | dynamic-update-slice | bytes 524292 | tf_op jit(solution)/shard_map/scatter-mul | solution.py:38
  1078.1 20.1 %fusion.50 = f32[64,8,8,128]{3,1,2,0:T(8,128)S(1)} fusion(f32[64,8,8,128]{3,1,2,0:T(8,128)} %fusion.82, f32[64,10,10,130]{3,1,2,0:T(8,128)} %scatter-mul.59, f32[64,8,8,128]{3,1,2,0:T(8,128)} %fusion.66, f32[]{:T(128)S(6)} %div.58, f32[]{:T(128)S(6)} %div.57, f32[8,8,128]{2,0,1:T(8,128)S(1)} %copy.200, f32[8,8,128]{2,0,1:T(8,128)S(1)} %copy.199, ...), kind=kLoop, calls=%fused_computation.77 | loop fusion | flops 12058624 | bytes 21200904 | tf_op jit(solution)/shard_map/sub | solution.py:86
  1170.6 87.4 %scatter-mul.60 = f32[64,10,10,130]{3,1,2,0:T(8,128)} dynamic-update-slice(f32[64,10,10,130]{3,1,2,0:T(8,128)} %pad_maximum_fusion.4, f32[64,1,8,128]{3,1,2,0:T(1,128)S(1)} %copy.242, s32[]{:T(128)} %constant.380.clone.1, s32[]{:T(128)} %constant.380.clone.1, s32[]{:T(128)} %constant.381.clone.1, s32[]{:T(128)} %constant.381.clone.1) | dynamic-update-slice | bytes 524292 | tf_op jit(solution)/shard_map/scatter-mul | solution.py:37
  1260.8 87.5 %scatter-mul.61 = f32[64,10,10,130]{3,1,2,0:T(8,128)} dynamic-update-slice(f32[64,10,10,130]{3,1,2,0:T(8,128)} %scatter-mul.60, f32[64,1,8,128]{3,1,2,0:T(1,128)S(1)} %slice_multiply_fusion.4, s32[]{:T(128)} %constant.380.clone.1, s32[]{:T(128)} %constant.383.clone.1, s32[]{:T(128)} %constant.381.clone.1, s32[]{:T(128)} %constant.381.clone.1) | dynamic-update-slice | bytes 524292 | tf_op jit(solution)/shard_map/scatter-mul | solution.py:38
  1348.3 20.1 %fusion.34 = f32[64,8,8,128]{3,1,2,0:T(8,128)} fusion(f32[64,8,8,128]{3,1,2,0:T(8,128)} %fusion.66, f32[64,10,10,130]{3,1,2,0:T(8,128)} %scatter-mul.61, f32[64,8,8,128]{3,1,2,0:T(8,128)S(1)} %fusion.50, f32[]{:T(128)S(6)} %div.58, f32[]{:T(128)S(6)} %div.57, f32[8,8,128]{2,0,1:T(8,128)S(1)} %copy.200, f32[8,8,128]{2,0,1:T(8,128)S(1)} %copy.199, ...), kind=kLoop, calls=%fused_computation.55 | loop fusion | flops 12058624 | bytes 21200904 | tf_op jit(solution)/shard_map/sub | solution.py:86
  1417.9 13.5 collective-permute-done.40
  1440.5 87.4 %scatter-mul.64 = f32[64,10,10,130]{3,1,2,0:T(8,128)} dynamic-update-slice(f32[64,10,10,130]{3,1,2,0:T(8,128)} %pad_maximum_fusion.5, f32[64,1,8,128]{3,1,2,0:T(1,128)S(1)} %copy.252, s32[]{:T(128)} %constant.380.clone.1, s32[]{:T(128)} %constant.380.clone.1, s32[]{:T(128)} %constant.381.clone.1, s32[]{:T(128)} %constant.381.clone.1) | dynamic-update-slice | bytes 524292 | tf_op jit(solution)/shard_map/scatter-mul | solution.py:37
  1530.8 87.5 %scatter-mul.65 = f32[64,10,10,130]{3,1,2,0:T(8,128)} dynamic-update-slice(f32[64,10,10,130]{3,1,2,0:T(8,128)} %scatter-mul.64, f32[64,1,8,128]{3,1,2,0:T(1,128)S(1)} %slice_multiply_fusion.2, s32[]{:T(128)} %constant.380.clone.1, s32[]{:T(128)} %constant.383.clone.1, s32[]{:T(128)} %constant.381.clone.1, s32[]{:T(128)} %constant.381.clone.1) | dynamic-update-slice | bytes 524292 | tf_op jit(solution)/shard_map/scatter-mul | solution.py:38
  1618.2 21.1 %broadcast_divide_fusion = (f32[64,8,8,128]{3,1,2,0:T(8,128)}, f32[64,8,8,128]{3,1,2,0:T(8,128)S(1)}) fusion(f32[8,8,128]{2,0,1:T(8,128)S(1)} %copy.183, f32[64,8,8,128]{3,1,2,0:T(8,128)} %copy-done, f32[]{:T(128)S(6)} %div.58, f32[64,8,8,128]{3,1,2,0:T(8,128)} %fusion.34, f32[]{:T(128)S(6)} %div.57, f32[64,10,10,130]{3,1,2,0:T(8,128)} %scatter-mul.65, ...), kind=kLoop, calls=%fused_computation.165 | loop fusion | flops 12582912 | bytes 23298056 | tf_op jit(solution)/shard_map/div | solution.py:88
  1711.3 87.4 %scatter-mul.66 = f32[64,10,10,130]{3,1,2,0:T(8,128)} dynamic-update-slice(f32[64,10,10,130]{3,1,2,0:T(8,128)} %pad_maximum_fusion.6, f32[64,1,8,128]{3,1,2,0:T(1,128)S(1)} %copy.268, s32[]{:T(128)} %constant.380.clone.1, s32[]{:T(128)} %constant.380.clone.1, s32[]{:T(128)} %constant.381.clone.1, s32[]{:T(128)} %constant.381.clone.1) | dynamic-update-slice | bytes 524292 | tf_op jit(solution)/shard_map/scatter-mul | solution.py:37
  1801.6 87.5 %scatter-mul.69 = f32[64,10,10,130]{3,1,2,0:T(8,128)} dynamic-update-slice(f32[64,10,10,130]{3,1,2,0:T(8,128)} %scatter-mul.66, f32[64,1,8,128]{3,1,2,0:T(1,128)S(1)} %slice_multiply_fusion, s32[]{:T(128)} %constant.380.clone.1, s32[]{:T(128)} %constant.383.clone.1, s32[]{:T(128)} %constant.381.clone.1, s32[]{:T(128)} %constant.381.clone.1) | dynamic-update-slice | bytes 524292 | tf_op jit(solution)/shard_map/scatter-mul | solution.py:38
  1889.0 19.3 fusion.2
  1913.9 60.5 %all-reduce = (f32[64,64]{0,1:T(8,128)S(1)}, f32[64,64]{0,1:T(8,128)S(1)}) all-reduce(f32[64,64]{0,1:T(8,128)S(1)} %fusion.113, f32[64,64]{0,1:T(8,128)S(1)} %fusion.118), channel_id=1, replica_groups=mesh['gx'=2,'gy'=4,'gz'=4] {'gy','gz'}, use_global_device_ids=true, to_apply=%region_4.5 | all-reduce | flops 8192 | bytes 65536 | tf_op jit(solution)/shard_map/psum | solution.py:92
  (281 shorter events, 549.6 us)
Async XLA Ops:
  2.8 17.3 collective-permute-start.1
  20.3 18.3 collective-permute-start.3
  32.9 16.9 collective-permute-start.7
  32.9 23.7 %collective-permute-start.8 = (f32[64,8,1,130]{3,1,2,0:T(8,128)}, f32[64,8,1,130]{3,1,2,0:T(8,128)S(1)}, u32[]{:S(2)}, u32[]{:S(2)}) collective-permute-start(f32[64,8,1,130]{3,1,2,0:T(8,128)} %get-tuple-element.217), channel_id=1, source_target_pairs={{4,0},{8,4},{12,8},{0,12},{5,1},{9,5},{13,9},{1,13},{6,2},{10,6},{... | collective-permute-start | bytes 798728 | tf_op jit(solution)/shard_map/ppermute | solution.py:18
  38.7 27.8 %collective-permute-start.4 = (f32[1,10,130]{2,1,0:T(8,128)S(1)}, f32[1,10,130]{2,1,0:T(8,128)S(1)}, u32[]{:S(2)}, u32[]{:S(2)}) collective-permute-start(f32[1,10,130]{2,1,0:T(8,128)S(1)} %get-tuple-element.234), channel_id=1, source_target_pairs={{1,0},{2,1},{3,2},{0,3},{5,4},{6,5},{7,6},{4,7},{9,8},{10,9},{11,1... | collective-permute-start | bytes 15608 | tf_op jit(solution)/shard_map/ppermute | solution.py:18
  38.7 27.7 %collective-permute-start.11 = (f32[1,10,130]{2,1,0:T(8,128)S(1)}, f32[1,10,130]{2,1,0:T(8,128)S(1)}, u32[]{:S(2)}, u32[]{:S(2)}) collective-permute-start(f32[1,10,130]{2,1,0:T(8,128)S(1)} %get-tuple-element.235), channel_id=1, source_target_pairs={{0,1},{1,2},{2,3},{3,0},{4,5},{5,6},{6,7},{7,4},{8,9},{9,10},{10,1... | collective-permute-start | bytes 15608 | tf_op jit(solution)/shard_map/ppermute | solution.py:15
  64.6 16.4 collective-permute-start.10
  303.1 16.8 collective-permute-start.14
  305.5 23.7 %collective-permute-start.15 = (f32[64,8,1,130]{3,1,2,0:T(8,128)S(1)}, f32[64,8,1,130]{3,1,2,0:T(8,128)S(1)}, u32[]{:S(2)}, u32[]{:S(2)}) collective-permute-start(f32[64,8,1,130]{3,1,2,0:T(8,128)S(1)} %get-tuple-element.215), channel_id=1, source_target_pairs={{4,0},{8,4},{12,8},{0,12},{5,1},{9,5},{13,9},{1,13},{6,2},{10,6},{... | collective-permute-start | bytes 798728 | tf_op jit(solution)/shard_map/ppermute | solution.py:18
  333.6 16.1 collective-permute-start.17
  575.8 16.7 collective-permute-start.20
  576.4 24.4 %collective-permute-start.21 = (f32[64,8,1,130]{3,1,2,0:T(8,128)S(1)}, f32[64,8,1,130]{3,1,2,0:T(8,128)S(1)}, u32[]{:S(2)}, u32[]{:S(2)}) collective-permute-start(f32[64,8,1,130]{3,1,2,0:T(8,128)S(1)} %get-tuple-element.213), channel_id=1, source_target_pairs={{4,0},{8,4},{12,8},{0,12},{5,1},{9,5},{13,9},{1,13},{6,2},{10,6},{... | collective-permute-start | bytes 798728 | tf_op jit(solution)/shard_map/ppermute | solution.py:18
  845.7 16.7 collective-permute-start.26
  847.0 24.6 %collective-permute-start.27 = (f32[64,8,1,130]{3,1,2,0:T(8,128)S(1)}, f32[64,8,1,130]{3,1,2,0:T(8,128)S(1)}, u32[]{:S(2)}, u32[]{:S(2)}) collective-permute-start(f32[64,8,1,130]{3,1,2,0:T(8,128)S(1)} %get-tuple-element.211), channel_id=1, source_target_pairs={{4,0},{8,4},{12,8},{0,12},{5,1},{9,5},{13,9},{1,13},{6,2},{10,6},{... | collective-permute-start | bytes 798728 | tf_op jit(solution)/shard_map/ppermute | solution.py:18
  876.0 16.4 collective-permute-start.29
  1116.4 16.7 collective-permute-start.32
  1117.9 24.1 %collective-permute-start.33 = (f32[64,8,1,130]{3,1,2,0:T(8,128)S(1)}, f32[64,8,1,130]{3,1,2,0:T(8,128)S(1)}, u32[]{:S(2)}, u32[]{:S(2)}) collective-permute-start(f32[64,8,1,130]{3,1,2,0:T(8,128)S(1)} %get-tuple-element.209), channel_id=1, source_target_pairs={{4,0},{8,4},{12,8},{0,12},{5,1},{9,5},{13,9},{1,13},{6,2},{10,6},{... | collective-permute-start | bytes 798728 | tf_op jit(solution)/shard_map/ppermute | solution.py:18
  1146.5 16.4 collective-permute-start.35
  1387.1 16.7 collective-permute-start.38
  1387.7 24.0 %collective-permute-start.39 = (f32[64,8,1,130]{3,1,2,0:T(8,128)S(1)}, f32[64,8,1,130]{3,1,2,0:T(8,128)S(1)}, u32[]{:S(2)}, u32[]{:S(2)}) collective-permute-start(f32[64,8,1,130]{3,1,2,0:T(8,128)S(1)} %get-tuple-element.207), channel_id=1, source_target_pairs={{4,0},{8,4},{12,8},{0,12},{5,1},{9,5},{13,9},{1,13},{6,2},{10,6},{... | collective-permute-start | bytes 798728 | tf_op jit(solution)/shard_map/ppermute | solution.py:18
  1416.1 16.4 collective-permute-start.41
  1657.6 16.7 collective-permute-start.44
  1658.8 24.1 %collective-permute-start.45 = (f32[64,8,1,130]{3,1,2,0:T(8,128)S(1)}, f32[64,8,1,130]{3,1,2,0:T(8,128)S(1)}, u32[]{:S(2)}, u32[]{:S(2)}) collective-permute-start(f32[64,8,1,130]{3,1,2,0:T(8,128)S(1)} %get-tuple-element.205), channel_id=1, source_target_pairs={{4,0},{8,4},{12,8},{0,12},{5,1},{9,5},{13,9},{1,13},{6,2},{10,6},{... | collective-permute-start | bytes 798728 | tf_op jit(solution)/shard_map/ppermute | solution.py:18
  1687.3 16.2 collective-permute-start.47
  (47 other events, 903.5 us)
